TPU v7x, 32 devices: a whole 2x2x4 slice. The times are simulated.
32 devices in a mesh: vid: 4 (over z), ty: 2 (over y), tx: 4 (over x, core).
Axes of the slice: x: 2, y: 2, z: 4, core: 2. Of those that a mesh axis runs over, the one named last changes fastest.
Arguments:
- latent_shards: bfloat16 [4, 99328], P('vid', ('ty', 'tx')), may hold values from -6 to 6
- shard_starts: int32 [4, 9], P('vid'), may hold values from 0 to 4096, as said below
- frame_dims: int32 [4, 2], P('vid'), may hold values from 16 to 128, as said below
- latent_cache: bfloat16 [4, 2, 32, 2048], P('vid', None, 'ty', 'tx'), may hold values from -6 to 6
- feature_cache: bfloat16 [4, 2, 32, 49152], P('vid', None, 'ty', 'tx'), may hold values from -5 to 5
- in_weight: bfloat16 [432, 384], replicated, may hold values from -0.3125 to 0.3125
- in_bias: float32 [384], replicated, may hold values from -3 to 3
- norm_gain: float32 [384], replicated, may hold values from 0.1 to 1.9
- res_weight: bfloat16 [10368, 384], replicated, may hold values from -0.0625 to 0.0625
- res_bias: float32 [384], replicated, may hold values from -3 to 3
- up_weight: bfloat16 [3456, 192], replicated, may hold values from -0.109375 to 0.109375
- up_bias: float32 [192], replicated, may hold values from -3 to 3
Outputs:
- decoded: bfloat16 [4, 64, 49152], P('vid', 'ty', 'tx')
Inputs may be any that keep to these rules, and one draw needn't show every extreme that they name: `frame_dims`: row i gives video i's height, from 16 to 32, and width, from 64 to 128; one video fills the whole canvas and another is exactly 16 by 64. `shard_starts`: row i starts at 0, never falls, ends at video i's height times width, and every shard's token count fits its 776 slots; tokens lie in row-major order of the frame.
All inputs are finite; a program needn't handle non-finite values.
Results may differ from a plain program's by a relative error of at most 0.0095.
Values may be sent and summed in bfloat16 or wider, within the bound.
A program may use at most 64 MiB of HBM per device.

v0:
```python
import jax
import jax.numpy as jnp
from jax import lax
from jax.sharding import PartitionSpec as P

EPS = 1e-06


def padded_2(value, sides, width):
    for axis, dim in sides:
        size, length = (lax.axis_size(axis), value.shape[dim])
        up = [(i, (i + 1) % size) for i in range(size - 1)]
        down = [(j, i) for i, j in up]
        last = lax.slice_in_dim(value, length - width, length, axis=dim)
        leading = lax.slice_in_dim(value, 0, width, axis=dim)
        before = lax.ppermute(last, axis, up)
        after = lax.ppermute(leading, axis, down)
        value = jnp.concatenate([before, value, after], axis=dim)
    return value


def tap_sum(padded, weight, row_count, col_count):
    channels = padded.shape[-1]
    summed = jnp.zeros((row_count * col_count, weight.shape[1]), jnp.float32)
    for frame_at in range(padded.shape[0]):
        for row_at in range(3):
            for col_at in range(3):
                tap_index = (frame_at * 3 + row_at) * 3 + col_at
                window = padded[
                    frame_at, row_at : row_at + row_count, col_at : col_at + col_count
                ].reshape(row_count * col_count, channels)
                summed = summed + jnp.dot(
                    window,
                    weight[tap_index * channels : (tap_index + 1) * channels],
                    preferred_element_type=jnp.float32,
                )
    return summed


def unfold_taps(padded, row_count, col_count):
    pieces = []
    for frame_at in range(padded.shape[0]):
        for row_at in range(3):
            for col_at in range(3):
                pieces.append(
                    padded[frame_at, row_at : row_at + row_count, col_at : col_at + col_count]
                )
    joined = jnp.concatenate(pieces, axis=-1)
    return joined.reshape(row_count * col_count, joined.shape[-1])


def token_routes(first, count, breadth, slot_cap, tile_rows, tile_cols, across, shard_count):
    offset = jnp.arange(slot_cap, dtype=jnp.int32)
    position = first[..., None] + offset
    live = offset < count[..., None]
    glob_row = position // breadth
    glob_col = position % breadth
    owner = jnp.where(live, glob_row // tile_rows * across + glob_col // tile_cols, shard_count)
    place = glob_row % tile_rows * tile_cols + glob_col % tile_cols
    return (owner, place)


def per_device(
    latent_shards,
    shard_starts,
    frame_dims,
    latent_cache,
    feature_cache,
    in_weight,
    in_bias,
    norm_gain,
    res_weight,
    res_bias,
    up_weight,
    up_bias,
):
    channels = in_bias.shape[0]
    latent_width = in_weight.shape[0] // 27
    out_width = up_bias.shape[0]
    tile_rows = feature_cache.shape[2]
    tile_cols = feature_cache.shape[3] // channels
    tile_cells = tile_rows * tile_cols
    across = lax.axis_size("tx")
    down_count = lax.axis_size("ty")
    shard_count = down_count * across
    row_index = lax.axis_index("ty")
    col_index = lax.axis_index("tx")
    myself = row_index * across + col_index
    height = frame_dims[0, 0]
    breadth = frame_dims[0, 1]
    starts = shard_starts[0]
    slot_cap = latent_shards.shape[1] // latent_width
    everything = lax.all_gather(latent_shards, ("ty", "tx"), axis=1, tiled=True).reshape(
        shard_count * slot_cap, latent_width
    )
    owner, place = token_routes(
        starts[:-1],
        starts[1:] - starts[:-1],
        breadth,
        slot_cap,
        tile_rows,
        tile_cols,
        across,
        shard_count,
    )
    target = jnp.where(owner == myself, place, tile_cells).reshape(-1)
    current = (
        jnp.zeros((tile_cells, latent_width), jnp.bfloat16).at[target].set(everything, mode="drop")
    )
    ycoord = row_index * tile_rows + jnp.arange(tile_rows, dtype=jnp.int32)
    xcoord = col_index * tile_cols + jnp.arange(tile_cols, dtype=jnp.int32)
    keep = ((ycoord[:, None] < height) & (xcoord[None, :] < breadth)).astype(jnp.float32)
    keep_low = keep.astype(jnp.bfloat16)[None, :, :, None]
    keep_flat = keep.reshape(-1, 1)
    lat_stack = (
        jnp.concatenate(
            [
                latent_cache[0].reshape(2, tile_rows, tile_cols, latent_width),
                current.reshape(1, tile_rows, tile_cols, latent_width),
            ],
            0,
        )
        * keep_low
    )
    lat_padded = padded_2(lat_stack, (("ty", 1), ("tx", 2)), 1)
    unfolded = unfold_taps(lat_padded, tile_rows, tile_cols)
    first_out = (jnp.dot(unfolded, in_weight, preferred_element_type=jnp.float32) + in_bias).astype(
        jnp.bfloat16
    )
    values = first_out.astype(jnp.float32)
    power = jnp.mean(values * values, axis=1, keepdims=True)
    normed = values * lax.rsqrt(power + EPS) * norm_gain
    hidden = (jax.nn.silu(normed) * keep_flat).astype(jnp.bfloat16)
    feat_stack = jnp.concatenate(
        [
            feature_cache[0].reshape(2, tile_rows, tile_cols, channels) * keep_low,
            hidden.reshape(1, tile_rows, tile_cols, channels),
        ],
        0,
    )
    feat_padded = padded_2(feat_stack, (("ty", 1), ("tx", 2)), 1)
    branch = tap_sum(feat_padded, res_weight, tile_rows, tile_cols)
    mixed = (
        ((values + branch + res_bias) * keep_flat)
        .astype(jnp.bfloat16)
        .reshape(tile_rows, tile_cols, channels)
    )
    low_padded = padded_2(mixed, (("ty", 0), ("tx", 1)), 1)
    grown_padded = jnp.repeat(jnp.repeat(low_padded, 2, axis=0), 2, axis=1)[1:-1, 1:-1]
    result = tap_sum(grown_padded[None], up_weight, 2 * tile_rows, 2 * tile_cols) + up_bias
    keep_high = jnp.repeat(jnp.repeat(keep, 2, axis=0), 2, axis=1).reshape(-1, 1)
    return (
        (result * keep_high)
        .astype(jnp.bfloat16)
        .reshape(1, 2 * tile_rows, 2 * tile_cols * out_width)
    )


def solution(mesh):
    return jax.shard_map(
        per_device,
        mesh=mesh,
        in_specs=(
            P("vid", ("ty", "tx")),
            P("vid", None),
            P("vid", None),
            P("vid", None, "ty", "tx"),
            P("vid", None, "ty", "tx"),
            P(),
            P(),
            P(),
            P(),
            P(),
            P(),
            P(),
        ),
        out_specs=P("vid", "ty", "tx"),
        check_vma=False,
    )
```

profile of v0, /device:TPU:1, one launch (start us, length us, event | category | flops | bytes accessed | tf_op | source)
XLA Modules:
  0.0 160.1 jit_solution(8422800603614920463)
XLA Ops:
  0.0 0.7 slice_bitcast_fusion.3
  0.7 0.8 bitcast_subtract_fusion
  1.5 1.3 fusion.105
  4.7 1.3 fusion.94
  6.2 1.0 fusion.95
  7.5 11.2 %all_gather.3 = bf16[1,99328]{1,0:T(2,128)(2,1)S(1)} all-gather(bf16[1,12416]{1,0:T(2,128)(2,1)} %param.12), channel_id=1, replica_groups=mesh['vid'=4,'ty'=2,'tx'=4] {'ty','tx'}, dimensions={1}, use_global_device_ids=true | all-gather | bytes 223488 | tf_op jit(solution)/shard_map/all_gather | solution.py:93
  18.7 1.2 reduce.1
  20.0 1.0 reshape.439
  21.0 0.6 add_compare_fusion
  21.8 0.7 add_compare_fusion.1
  23.1 24.5 %scatter_custom_fusion = bf16[512,16]{1,0:T(8,128)(2,1)S(1)} fusion(s32[6208]{0:T(1024)S(1)} %fusion.97, bf16[6208,16]{1,0:T(8,128)(2,1)S(1)} %reshape.439, bf16[]{:T(256)} %constant.70.clone.1), kind=kCustom, calls=%fused_computation.159 | custom fusion | bytes 16386 | tf_op jit(solution)/shard_map/scatter | solution.py:108
  47.8 2.9 %collective-permute-start = (bf16[3,1,32,16]{3,2,1,0:T(8,128)(2,1)S(1)}, bf16[3,1,32,16]{3,2,1,0:T(8,128)(2,1)S(1)}, u32[]{:S(2)}, u32[]{:S(2)}) collective-permute-start(bf16[3,1,32,16]{3,2,1,0:T(8,128)(2,1)S(1)} %get-tuple-element.84), channel_id=1, source_target_pairs={{0,4},{1,5},{2,6},{3,7},{8,12},{9,13},{10,14},{11,15},{16,20},{17,... | collective-permute-start | bytes 9224 | tf_op jit(solution)/shard_map/ppermute | solution.py:16
  50.6 1.3 collective-permute-start.1
  52.3 1.4 fusion.72
  53.7 1.5 collective-permute-done.1
  55.3 0.7 fusion.103
  56.2 3.5 %collective-permute-start.3 = (bf16[3,18,1,16]{3,2,1,0:T(2,128)(2,1)}, bf16[3,18,1,16]{3,2,1,0:T(2,128)(2,1)}, u32[]{:S(2)}, u32[]{:S(2)}) collective-permute-start(bf16[3,18,1,16]{3,2,1,0:T(2,128)(2,1)} %get-tuple-element.68), channel_id=1, source_target_pairs={{1,0},{2,1},{3,2},{5,4},{6,5},{7,6},{9,8},{10,9},{11,10},{13,12},{... | collective-permute-start | bytes 5192 | tf_op jit(solution)/shard_map/ppermute | solution.py:17
  59.7 2.5 %collective-permute-start.2 = (bf16[3,18,1,16]{3,2,1,0:T(2,128)(2,1)}, bf16[3,18,1,16]{3,2,1,0:T(2,128)(2,1)}, u32[]{:S(2)}, u32[]{:S(2)}) collective-permute-start(bf16[3,18,1,16]{3,2,1,0:T(2,128)(2,1)} %get-tuple-element.69), channel_id=1, source_target_pairs={{0,1},{1,2},{2,3},{4,5},{5,6},{6,7},{8,9},{9,10},{10,11},{12,13},{... | collective-permute-start | bytes 5192 | tf_op jit(solution)/shard_map/ppermute | solution.py:16
  62.2 0.8 pad_maximum_fusion.11
  63.0 1.6 copy.41
  64.5 1.0 copy.42
  66.1 1.2 copy.23
  67.7 0.7 concatenate.149
  68.4 1.2 copy.19
  70.0 0.6 constant_dynamic-update-slice_fusion.26
  72.9 0.6 constant_dynamic-update-slice_fusion.25
  73.5 0.6 constant_dynamic-update-slice_fusion.24
  74.1 0.6 constant_dynamic-update-slice_fusion.23
  74.7 0.6 constant_dynamic-update-slice_fusion.22
  75.4 0.6 constant_dynamic-update-slice_fusion.21
  88.7 1.7 %multiply_reduce_fusion = (f32[512]{0:T(512)S(1)}, f32[512,384]{1,0:T(8,128)S(1)}) fusion(f32[384]{0:T(512)S(1)} %copy-done.16, bf16[512,432]{0,1:T(8,128)(2,1)} %constant_dynamic-update-slice_fusion, bf16[432,384]{1,0:T(8,128)(2,1)S(1)} %copy-done), kind=kOutput, calls=%fused_computation.50 | convolution fusion | flops 170851840 | bytes 1564160 | tf_op jit(solution)/shard_map/dot_general | solution.py:127
  90.8 2.3 %collective-permute-start.4 = (bf16[3,1,32,384]{3,2,1,0:T(8,128)(2,1)S(1)}, bf16[3,1,32,384]{3,2,1,0:T(8,128)(2,1)S(1)}, u32[]{:S(2)}, u32[]{:S(2)}) collective-permute-start(bf16[3,1,32,384]{3,2,1,0:T(8,128)(2,1)S(1)} %get-tuple-element.45), channel_id=1, source_target_pairs={{0,4},{1,5},{2,6},{3,7},{8,12},{9,13},{10,14},{11,15},{16,20},{17,... | collective-permute-start | bytes 221192 | tf_op jit(solution)/shard_map/ppermute | solution.py:16
  93.1 1.3 collective-permute-start.5
  94.4 1.4 fusion.38
  95.7 2.9 %collective-permute-done.5 = bf16[3,1,32,384]{3,2,1,0:T(8,128)(2,1)S(1)} collective-permute-done((bf16[3,1,32,384]{3,2,1,0:T(8,128)(2,1)S(1)}, bf16[3,1,32,384]{3,2,1,0:T(8,128)(2,1)S(1)}, u32[]{:S(2)}, u32[]{:S(2)}) %collective-permute-start.5) | collective-permute-done | bytes 73760 | tf_op jit(solution)/shard_map/ppermute | solution.py:17
  99.0 1.4 fusion.78
  100.5 3.3 %collective-permute-start.6 = (bf16[3,18,1,384]{3,2,1,0:T(2,128)(2,1)S(1)}, bf16[3,18,1,384]{3,2,1,0:T(2,128)(2,1)S(1)}, u32[]{:S(2)}, u32[]{:S(2)}) collective-permute-start(bf16[3,18,1,384]{3,2,1,0:T(2,128)(2,1)S(1)} %get-tuple-element.34), channel_id=1, source_target_pairs={{0,1},{1,2},{2,3},{4,5},{5,6},{6,7},{8,9},{9,10},{10,11},{12,13},{... | collective-permute-start | bytes 124424 | tf_op jit(solution)/shard_map/ppermute | solution.py:16
  103.8 2.1 %collective-permute-start.7 = (bf16[3,18,1,384]{3,2,1,0:T(2,128)(2,1)S(1)}, bf16[3,18,1,384]{3,2,1,0:T(2,128)(2,1)S(1)}, u32[]{:S(2)}, u32[]{:S(2)}) collective-permute-start(bf16[3,18,1,384]{3,2,1,0:T(2,128)(2,1)S(1)} %get-tuple-element.35), channel_id=1, source_target_pairs={{1,0},{2,1},{3,2},{5,4},{6,5},{7,6},{9,8},{10,9},{11,10},{13,12},{... | collective-permute-start | bytes 124424 | tf_op jit(solution)/shard_map/ppermute | solution.py:17
  106.0 1.4 fusion.55
  109.0 1.3 fusion.33
  110.3 1.9 %maximum_maximum_fusion = (bf16[3,18,33,384]{3,2,1,0:T(8,128)(2,1)S(1)}, bf16[3,18,33,384]{3,2,1,0:T(8,128)(2,1)S(1)}) fusion(bf16[3,1,32,384]{3,2,1,0:T(8,128)(2,1)S(1)} %collective-permute-done.5, bf16[1,16,32,384]{3,2,1,0:T(8,128)(2,1)S(1)} %bitcast.185, bf16[2,16,32,384]{3,2,1,0:T(8,128)(2,1)S(1)} %bitcast_multiply_fusion, ...), kind=kLoop, calls=%fused_computation.13 | loop fusion | flops 13685760 | bytes 4147200 | tf_op jit(solution)/shard_map/concatenate | solution.py:18
  112.2 2.0 %fusion.101 = (bf16[1,16,32,384]{3,2,1,0:T(8,128)(2,1)}, bf16[1,16,32,384]{3,2,1,0:T(8,128)(2,1)}, bf16[1,16,32,384]{3,2,1,0:T(8,128)(2,1)S(1)}, bf16[1,16,32,38...) fusion(bf16[3,18,33,384]{3,2,1,0:T(8,128)(2,1)S(1)} %get-tuple-, ...), kind=kLoop, calls=%fused_computation.218 | loop fusion | bytes 14155776 | tf_op jit(solution)/shard_map/slice | solution.py:29
  120.7 0.8 fusion.13
  121.5 0.8 fusion.21
  123.3 1.4 collective-permute-start.8
  124.8 1.3 collective-permute-start.9
  126.1 3.3 %collective-permute-done.9 = bf16[1,32,384]{2,1,0:T(8,128)(2,1)S(1)} collective-permute-done((bf16[1,32,384]{2,1,0:T(8,128)(2,1)S(1)}, bf16[1,32,384]{2,1,0:T(8,128)(2,1)S(1)}, u32[]{:S(2)}, u32[]{:S(2)}) %collective-permute-start.9) | collective-permute-done | bytes 24608 | tf_op jit(solution)/shard_map/ppermute | solution.py:17
  129.4 5.1 %collective-permute-start.10 = (bf16[18,1,384]{2,1,0:T(2,128)(2,1)S(1)}, bf16[18,1,384]{2,1,0:T(2,128)(2,1)S(1)}, u32[]{:S(2)}, u32[]{:S(2)}) collective-permute-start(bf16[18,1,384]{2,1,0:T(2,128)(2,1)S(1)} %get-tuple-element.48), channel_id=1, source_target_pairs={{0,1},{1,2},{2,3},{4,5},{5,6},{6,7},{8,9},{9,10},{10,11},{12,13},{... | collective-permute-start | bytes 41480 | tf_op jit(solution)/shard_map/ppermute | solution.py:16
  134.5 2.2 %collective-permute-start.11 = (bf16[18,1,384]{2,1,0:T(2,128)(2,1)S(1)}, bf16[18,1,384]{2,1,0:T(2,128)(2,1)S(1)}, u32[]{:S(2)}, u32[]{:S(2)}) collective-permute-start(bf16[18,1,384]{2,1,0:T(2,128)(2,1)S(1)} %get-tuple-element.49), channel_id=1, source_target_pairs={{1,0},{2,1},{3,2},{5,4},{6,5},{7,6},{9,8},{10,9},{11,10},{13,12},{... | collective-permute-start | bytes 41480 | tf_op jit(solution)/shard_map/ppermute | solution.py:17
  137.2 2.5 %collective-permute-done.11 = bf16[18,1,384]{2,1,0:T(2,128)(2,1)S(1)} collective-permute-done((bf16[18,1,384]{2,1,0:T(2,128)(2,1)S(1)}, bf16[18,1,384]{2,1,0:T(2,128)(2,1)S(1)}, u32[]{:S(2)}, u32[]{:S(2)}) %collective-permute-start.11) | collective-permute-done | bytes 13856 | tf_op jit(solution)/shard_map/ppermute | solution.py:17
  140.0 2.2 %broadcast_in_dim.42 = bf16[36,34,2,384]{3,2,1,0:T(2,128)(2,1)} broadcast(bf16[36,34,384]{2,1,0:T(8,128)(2,1)S(1)} %bitcast.197), dimensions={0,1,3} | broadcast | bytes 2820096 | tf_op jit(solution)/shard_map/broadcast_in_dim | solution.py:149
  142.2 4.2 %reshape.431 = bf16[36,68,384]{2,1,0:T(8,128)(2,1)S(1)} reshape(bf16[36,34,2,384]{3,2,1,0:T(2,128)(2,1)} %broadcast_in_dim.42) | data formatting | bytes 3760128 | tf_op jit(solution)/shard_map/reshape | solution.py:149
  146.4 0.9 slice_bitcast_fusion
  147.3 3.6 %fusion.100 = (bf16[1,32,64,384]{3,2,1,0:T(8,128)(2,1)S(1)}, bf16[1,32,64,384]{3,2,1,0:T(8,128)(2,1)S(1)}, bf16[1,32,64,384]{3,2,1,0:T(8,128)(2,1)S(1)}, bf16[1,...) fusion(bf16[1,34,66,384]{3,2,1,0:T(8,128)(2,1)S(1)} %slice_bitc, ...), kind=kLoop, calls=%fused_computation.217 | loop fusion | bytes 28311552 | tf_op jit(solution)/shard_map/slice | solution.py:29
  150.9 0.7 fusion.89
  151.6 0.7 convolution_add_fusion.7
  152.4 0.7 convolution_add_fusion.6
  153.1 0.7 convolution_add_fusion.5
  153.8 0.7 convolution_add_fusion.4
  154.6 0.7 convolution_add_fusion.3
  155.3 0.7 convolution_add_fusion.2
  156.0 0.7 convolution_add_fusion.1
  156.8 0.7 fusion.2
  158.0 2.1 %reshape.433 = bf16[1,32,12288]{2,1,0:T(8,128)(2,1)} reshape(bf16[2048,192]{1,0:T(8,128)(2,1)S(1)} %copy.50) | data formatting | bytes 1572864 | tf_op jit(solution)/shard_map/reshape | solution.py:155
  (161 shorter events, 29.8 us)
Async XLA Ops:
  0.0 88.7 %copy-start = (bf16[432,384]{1,0:T(8,128)(2,1)S(1)}, bf16[432,384]{1,0:T(8,128)(2,1)}, u32[]{:S(2)}) copy-start(bf16[432,384]{1,0:T(8,128)(2,1)} %param.17) | copy-start | bytes 995332
  0.0 21.6 %copy-start.12 = (bf16[1,2,16,512]{3,2,1,0:T(8,128)(2,1)S(1)}, bf16[1,2,16,512]{3,2,1,0:T(8,128)(2,1)}, u32[]{:S(2)}) copy-start(bf16[1,2,16,512]{3,2,1,0:T(8,128)(2,1)} %param.15) | copy-start | bytes 98308
  20.0 32.0 %copy-start.9 = (bf16[1,2,16,12288]{3,2,1,0:T(8,128)(2,1)S(1)}, bf16[1,2,16,12288]{3,2,1,0:T(8,128)(2,1)}, u32[]{:S(2)}) copy-start(bf16[1,2,16,12288]{3,2,1,0:T(8,128)(2,1)} %param.16) | copy-start | bytes 2359300
  47.8 6.0 %collective-permute-start = (bf16[3,1,32,16]{3,2,1,0:T(8,128)(2,1)S(1)}, bf16[3,1,32,16]{3,2,1,0:T(8,128)(2,1)S(1)}, u32[]{:S(2)}, u32[]{:S(2)}) collective-permute-start(bf16[3,1,32,16]{3,2,1,0:T(8,128)(2,1)S(1)} %get-tuple-element.84), channel_id=1, source_target_pairs={{0,4},{1,5},{2,6},{3,7},{8,12},{9,13},{10,14},{11,15},{16,20},{17,... | collective-permute-start | bytes 9224 | tf_op jit(solution)/shard_map/ppermute | solution.py:16
  50.6 4.6 %collective-permute-start.1 = (bf16[3,1,32,16]{3,2,1,0:T(8,128)(2,1)S(1)}, bf16[3,1,32,16]{3,2,1,0:T(8,128)(2,1)S(1)}, u32[]{:S(2)}, u32[]{:S(2)}) collective-permute-start(bf16[3,1,32,16]{3,2,1,0:T(8,128)(2,1)S(1)} %get-tuple-element.85), channel_id=1, source_target_pairs={{4,0},{5,1},{6,2},{7,3},{12,8},{13,9},{14,10},{15,11},{20,16},{21,... | collective-permute-start | bytes 9224 | tf_op jit(solution)/shard_map/ppermute | solution.py:17
  56.2 9.9 %collective-permute-start.3 = (bf16[3,18,1,16]{3,2,1,0:T(2,128)(2,1)}, bf16[3,18,1,16]{3,2,1,0:T(2,128)(2,1)}, u32[]{:S(2)}, u32[]{:S(2)}) collective-permute-start(bf16[3,18,1,16]{3,2,1,0:T(2,128)(2,1)} %get-tuple-element.68), channel_id=1, source_target_pairs={{1,0},{2,1},{3,2},{5,4},{6,5},{7,6},{9,8},{10,9},{11,10},{13,12},{... | collective-permute-start | bytes 5192 | tf_op jit(solution)/shard_map/ppermute | solution.py:17
  59.7 8.7 %collective-permute-start.2 = (bf16[3,18,1,16]{3,2,1,0:T(2,128)(2,1)}, bf16[3,18,1,16]{3,2,1,0:T(2,128)(2,1)}, u32[]{:S(2)}, u32[]{:S(2)}) collective-permute-start(bf16[3,18,1,16]{3,2,1,0:T(2,128)(2,1)} %get-tuple-element.69), channel_id=1, source_target_pairs={{0,1},{1,2},{2,3},{4,5},{5,6},{6,7},{8,9},{9,10},{10,11},{12,13},{... | collective-permute-start | bytes 5192 | tf_op jit(solution)/shard_map/ppermute | solution.py:16
  70.8 2.2 %copy-start.10 = (bf16[512,16]{0,1:T(8,128)(2,1)S(1)}, bf16[512,16]{0,1:T(8,128)(2,1)}, u32[]{:S(2)}) copy-start(bf16[512,16]{0,1:T(8,128)(2,1)} %copy.41) | copy-start | bytes 49156
  70.8 2.8 %copy-start.11 = (bf16[512,16]{0,1:T(8,128)(2,1)S(1)}, bf16[512,16]{0,1:T(8,128)(2,1)}, u32[]{:S(2)}) copy-start(bf16[512,16]{0,1:T(8,128)(2,1)} %concatenate.149) | copy-start | bytes 49156
  71.3 17.4 %copy-start.16 = (f32[384]{0:T(512)S(1)}, f32[384]{0:T(512)}, u32[]{:S(2)}) copy-start(f32[384]{0:T(512)} %param.18) | copy-start | bytes 4612
  72.6 17.8 %copy-start.13 = (f32[384]{0:T(512)S(1)}, f32[384]{0:T(512)}, u32[]{:S(2)}) copy-start(f32[384]{0:T(512)} %param.19) | copy-start | bytes 4612
  88.7 18.6 %slice-start = ((s8[7962624]{0:T(1024)(128)(4,1)}), s8[4194304]{0:T(1024)(128)(4,1)S(1)}, s32[]{:S(2)}) async-start(s8[7962624]{0:T(1024)(128)(4,1)} %bitcast.186), calls=%async_computation | async-start | bytes 8388608
  90.8 4.9 %collective-permute-start.4 = (bf16[3,1,32,384]{3,2,1,0:T(8,128)(2,1)S(1)}, bf16[3,1,32,384]{3,2,1,0:T(8,128)(2,1)S(1)}, u32[]{:S(2)}, u32[]{:S(2)}) collective-permute-start(bf16[3,1,32,384]{3,2,1,0:T(8,128)(2,1)S(1)} %get-tuple-element.45), channel_id=1, source_target_pairs={{0,4},{1,5},{2,6},{3,7},{8,12},{9,13},{10,14},{11,15},{16,20},{17,... | collective-permute-start | bytes 221192 | tf_op jit(solution)/shard_map/ppermute | solution.py:16
  93.1 5.6 %collective-permute-start.5 = (bf16[3,1,32,384]{3,2,1,0:T(8,128)(2,1)S(1)}, bf16[3,1,32,384]{3,2,1,0:T(8,128)(2,1)S(1)}, u32[]{:S(2)}, u32[]{:S(2)}) collective-permute-start(bf16[3,1,32,384]{3,2,1,0:T(8,128)(2,1)S(1)} %get-tuple-element.46), channel_id=1, source_target_pairs={{4,0},{5,1},{6,2},{7,3},{12,8},{13,9},{14,10},{15,11},{20,16},{21,... | collective-permute-start | bytes 221192 | tf_op jit(solution)/shard_map/ppermute | solution.py:17
  95.7 11.6 %slice-start.1 = ((s8[7962624]{0:T(1024)(128)(4,1)}), s8[3768320]{0:T(1024)(128)(4,1)S(1)}, s32[]{:S(2)}) async-start(s8[7962624]{0:T(1024)(128)(4,1)} %bitcast.186), calls=%async_computation.1 | async-start | bytes 7536640
  100.5 9.7 %collective-permute-start.6 = (bf16[3,18,1,384]{3,2,1,0:T(2,128)(2,1)S(1)}, bf16[3,18,1,384]{3,2,1,0:T(2,128)(2,1)S(1)}, u32[]{:S(2)}, u32[]{:S(2)}) collective-permute-start(bf16[3,18,1,384]{3,2,1,0:T(2,128)(2,1)S(1)} %get-tuple-element.34), channel_id=1, source_target_pairs={{0,1},{1,2},{2,3},{4,5},{5,6},{6,7},{8,9},{9,10},{10,11},{12,13},{... | collective-permute-start | bytes 124424 | tf_op jit(solution)/shard_map/ppermute | solution.py:16
  103.8 6.4 %collective-permute-start.7 = (bf16[3,18,1,384]{3,2,1,0:T(2,128)(2,1)S(1)}, bf16[3,18,1,384]{3,2,1,0:T(2,128)(2,1)S(1)}, u32[]{:S(2)}, u32[]{:S(2)}) collective-permute-start(bf16[3,18,1,384]{3,2,1,0:T(2,128)(2,1)S(1)} %get-tuple-element.35), channel_id=1, source_target_pairs={{1,0},{2,1},{3,2},{5,4},{6,5},{7,6},{9,8},{10,9},{11,10},{13,12},{... | collective-permute-start | bytes 124424 | tf_op jit(solution)/shard_map/ppermute | solution.py:17
  117.8 1.0 copy-start.7
  118.2 1.0 copy-start.6
  118.6 1.1 copy-start.5
  119.2 1.0 copy-start.4
  121.5 1.1 copy-start.2
  121.5 1.2 copy-start.3
  121.5 1.2 copy-start.14
  123.3 2.7 %collective-permute-start.8 = (bf16[1,32,384]{2,1,0:T(8,128)(2,1)S(1)}, bf16[1,32,384]{2,1,0:T(8,128)(2,1)S(1)}, u32[]{:S(2)}, u32[]{:S(2)}) collective-permute-start(bf16[1,32,384]{2,1,0:T(8,128)(2,1)S(1)} %get-tuple-element.76), channel_id=1, source_target_pairs={{0,4},{1,5},{2,6},{3,7},{8,12},{9,13},{10,14},{11,15},{16,20},{17,... | collective-permute-start | bytes 73736 | tf_op jit(solution)/shard_map/ppermute | solution.py:16
  124.8 4.6 %collective-permute-start.9 = (bf16[1,32,384]{2,1,0:T(8,128)(2,1)S(1)}, bf16[1,32,384]{2,1,0:T(8,128)(2,1)S(1)}, u32[]{:S(2)}, u32[]{:S(2)}) collective-permute-start(bf16[1,32,384]{2,1,0:T(8,128)(2,1)S(1)} %get-tuple-element.77), channel_id=1, source_target_pairs={{4,0},{5,1},{6,2},{7,3},{12,8},{13,9},{14,10},{15,11},{20,16},{21,... | collective-permute-start | bytes 73736 | tf_op jit(solution)/shard_map/ppermute | solution.py:17
  129.4 7.8 %collective-permute-start.10 = (bf16[18,1,384]{2,1,0:T(2,128)(2,1)S(1)}, bf16[18,1,384]{2,1,0:T(2,128)(2,1)S(1)}, u32[]{:S(2)}, u32[]{:S(2)}) collective-permute-start(bf16[18,1,384]{2,1,0:T(2,128)(2,1)S(1)} %get-tuple-element.48), channel_id=1, source_target_pairs={{0,1},{1,2},{2,3},{4,5},{5,6},{6,7},{8,9},{9,10},{10,11},{12,13},{... | collective-permute-start | bytes 41480 | tf_op jit(solution)/shard_map/ppermute | solution.py:16
  134.5 5.2 %collective-permute-start.11 = (bf16[18,1,384]{2,1,0:T(2,128)(2,1)S(1)}, bf16[18,1,384]{2,1,0:T(2,128)(2,1)S(1)}, u32[]{:S(2)}, u32[]{:S(2)}) collective-permute-start(bf16[18,1,384]{2,1,0:T(2,128)(2,1)S(1)} %get-tuple-element.49), channel_id=1, source_target_pairs={{1,0},{2,1},{3,2},{5,4},{6,5},{7,6},{9,8},{10,9},{11,10},{13,12},{... | collective-permute-start | bytes 41480 | tf_op jit(solution)/shard_map/ppermute | solution.py:17
  147.3 3.6 %copy-start.8 = (bf16[3456,192]{0,1:T(8,128)(2,1)S(1)}, bf16[3456,192]{0,1:T(8,128)(2,1)}, u32[]{:S(2)}) copy-start(bf16[3456,192]{0,1:T(8,128)(2,1)} %param.22) | copy-start | bytes 3981316
  156.0 0.7 copy-start.15
  156.8 3.3 %copy-start.1 = (bf16[432,384]{1,0:T(8,128)(2,1)S(1)}, bf16[432,384]{1,0:T(8,128)(2,1)}, u32[]{:S(2)}) copy-start(bf16[432,384]{1,0:T(8,128)(2,1)} %param.17) | copy-start | bytes 995332
where the time goes:
time: 161 us; the launch traced here: 160 us
  local copies, waits for them, and re-layouts  71.1 us (44%)
  starting transfers between devices  29.1 us (18%)
  matrix products  24.5 us (15%)
  blocking collectives  11.2 us (7%)
  other arithmetic  11.1 us (7%)
  waiting for transfers between devices  10.2 us (6%)
  between operations  2.86 us (2%)
    scatter x1, local copies, waits for them, and re-layouts, per_device(): jnp.zeros((tile_cells, latent_width), jnp.bfloat16).at[target]  24.5 us
    dot_general x36, matrix products, tap_sum(): jnp.dot(window, weight[tap_index * channels:(tap_index + 1) * channels],...  22.8 us
    ppermute x6, starting transfers between devices, padded_2(): before = lax.ppermute(last, axis, up)  17.4 us
    unnamed x65, local copies, waits for them, and re-layouts  16.8 us
    ppermute x6, starting transfers between devices, padded_2(): after = lax.ppermute(leading, axis, down)  11.7 us
    all_gather x1, blocking collectives, per_device(): lax.all_gather(latent_shards, ('ty', 'tx'), axis=1, tiled=True)  11.2 us
    ppermute x6, waiting for transfers between devices, padded_2(): after = lax.ppermute(leading, axis, down)  10.2 us
    concatenate x28, local copies, waits for them, and re-layouts, unfold_taps(): joined = jnp.concatenate(pieces, axis=-1)  6.48 us
  transfers between devices with their start and end apart: 12, of which 4 were waited for; matrix products, arithmetic and copies ran while one was open for 9% of the time, Pallas kernels for 0%

commit v1 on v0

--- a/solution.py
+++ b/solution.py
@@ -4,6 +4,18 @@
 from jax.sharding import PartitionSpec as P
 
 EPS = 1e-06
+
+
+def collect(x, axis, dim):
+    ways, here, step = (lax.axis_size(axis), lax.axis_index(axis), x.shape[dim])
+    line, have = (x, 1)
+    while have < ways:
+        line = jnp.concatenate(
+            [line, lax.ppermute(line, axis, [(d, (d - have) % ways) for d in range(ways)])],
+            axis=dim,
+        )
+        have = 2 * have
+    return jnp.roll(line, here * step, axis=dim)
 
 
 def padded_2(value, sides, width):
@@ -90,7 +102,7 @@
     breadth = frame_dims[0, 1]
     starts = shard_starts[0]
     slot_cap = latent_shards.shape[1] // latent_width
-    everything = lax.all_gather(latent_shards, ("ty", "tx"), axis=1, tiled=True).reshape(
+    everything = collect(latent_shards, ("ty", "tx"), 1).reshape(
         shard_count * slot_cap, latent_width
     )
     owner, place = token_routes(

time: 161 us -> 150 us (0.932)
  blocking collectives: 11.2 us -> 0 us
  local copies, waits for them, and re-layouts: 71.1 us -> 61.3 us
  starting transfers between devices: 29.1 us -> 37 us
  waiting for transfers between devices: 10.2 us -> 15 us
    all_gather x1 -> x0, blocking collectives: 11.2 us -> none  [per_device(): lax.all_gather(latent_shards, ('ty', 'tx'), axis=1, tiled=True)]
    unnamed x65 -> x78, local copies, waits for them, and re-layouts: 16.8 us -> 9.48 us
    ppermute x0 -> x3, waiting for transfers between devices: none -> 4.92 us  [collect(): lax.ppermute(line, axis, [(d, (d - have) % ways) for d in range(ways)])]
    ppermute x0 -> x3, starting transfers between devices: none -> 4.14 us  [collect(): lax.ppermute(line, axis, [(d, (d - have) % ways) for d in range(ways)])]
    concatenate x28, local copies, waits for them, and re-layouts: 6.48 us -> 2.88 us  [unfold_taps(): joined = jnp.concatenate(pieces, axis=-1)]
    ppermute x6, starting transfers between devices: 11.7 us -> 14.5 us  [padded_2(): after = lax.ppermute(leading, axis, down)]
    dynamic_slice x0 -> x1, local copies, waits for them, and re-layouts: none -> 2.11 us  [collect(): return jnp.roll(line, here * step, axis=dim)]
    slice x3 -> x4, local copies, waits for them, and re-layouts: 5.63 us -> 5.81 us  [tap_sum(): padded[frame_at, row_at:row_at + row_count, col_at:col_at + col_count]]
  transfers between devices with their start and end apart: 12 -> 15, of which waited for: 4 -> 6; matrix products, arithmetic and copies ran while one was open for 9% -> 14% of each run, Pallas kernels for 0% -> 0%
where the time goes in v1:
time: 150 us; the launch traced here: 149 us
  local copies, waits for them, and re-layouts  61.3 us (41%)
  starting transfers between devices  37 us (25%)
  matrix products  23.4 us (16%)
  waiting for transfers between devices  15 us (10%)
  other arithmetic  9.59 us (6%)
  between operations  3.23 us (2%)
    scatter x1, local copies, waits for them, and re-layouts, per_device(): jnp.zeros((tile_cells, latent_width), jnp.bfloat16).at[target]  24.5 us
    dot_general x36, matrix products, tap_sum(): jnp.dot(window, weight[tap_index * channels:(tap_index + 1) * channels],...  22.8 us
    ppermute x6, starting transfers between devices, padded_2(): before = lax.ppermute(last, axis, up)  18.4 us
    ppermute x6, starting transfers between devices, padded_2(): after = lax.ppermute(leading, axis, down)  14.5 us
    ppermute x6, waiting for transfers between devices, padded_2(): after = lax.ppermute(leading, axis, down)  10 us
    unnamed x78, local copies, waits for them, and re-layouts  9.48 us
    slice x4, local copies, waits for them, and re-layouts, tap_sum(): padded[frame_at, row_at:row_at + row_count, col_at:col_at + col_count]  5.81 us
    ppermute x3, waiting for transfers between devices, collect(): lax.ppermute(line, axis, [(d, (d - have) % ways) for d in range(ways)])  4.92 us
  transfers between devices with their start and end apart: 15, of which 6 were waited for; matrix products, arithmetic and copies ran while one was open for 14% of the time, Pallas kernels for 0%

profile of v1, /device:TPU:1, one launch (start us, length us, event | category | flops | bytes accessed | tf_op | source)
XLA Modules:
  0.0 149.5 jit_solution(12289595065302862377)
XLA Ops:
  0.1 1.5 %constant_dynamic-update-slice_fusion.7 = bf16[1,198656]{1,0:T(2,128)(2,1)} fusion(bf16[1,12416]{1,0:T(2,128)(2,1)} %param.12), kind=kLoop, calls=%fused_computation.149 | loop fusion | bytes 74496
  1.6 0.7 slice_bitcast_fusion.3
  2.2 0.8 bitcast_subtract_fusion
  3.0 1.4 fusion.105
  6.3 1.3 fusion.94
  7.8 1.0 fusion.95
  9.2 0.6 add_compare_fusion
  9.9 1.2 copy.51
  11.1 0.7 add_compare_fusion.1
  13.0 3.6 %collective-permute-start.1 = (bf16[1,24832]{1,0:T(2,128)(2,1)S(1)}, bf16[1,24832]{1,0:T(2,128)(2,1)S(1)}, u32[]{:S(2)}, u32[]{:S(2)}) collective-permute-start(bf16[1,24832]{1,0:T(2,128)(2,1)S(1)} %pad_maximum_fusion.18), channel_id=1, source_target_pairs={{0,6},{1,7},{2,0},{3,1},{4,2},{5,3},{6,4},{7,5},{8,14},{9,15},{10,... | collective-permute-start | bytes 149000 | tf_op jit(solution)/shard_map/ppermute | solution.py:14
  16.6 0.7 constant_dynamic-update-slice_fusion.6
  17.3 1.5 %collective-permute-done.1 = bf16[1,24832]{1,0:T(2,128)(2,1)S(1)} collective-permute-done((bf16[1,24832]{1,0:T(2,128)(2,1)S(1)}, bf16[1,24832]{1,0:T(2,128)(2,1)S(1)}, u32[]{:S(2)}, u32[]{:S(2)}) %collective-permute-start.1) | collective-permute-done | bytes 49696 | tf_op jit(solution)/shard_map/ppermute | solution.py:14
  19.5 0.7 constant_dynamic-update-slice_fusion.5
  20.2 3.4 %collective-permute-done.2 = bf16[1,49664]{1,0:T(2,128)(2,1)S(1)} collective-permute-done((bf16[1,49664]{1,0:T(2,128)(2,1)S(1)}, bf16[1,49664]{1,0:T(2,128)(2,1)S(1)}, u32[]{:S(2)}, u32[]{:S(2)}) %collective-permute-start.2) | collective-permute-done | bytes 99360 | tf_op jit(solution)/shard_map/ppermute | solution.py:14
  23.6 0.9 constant_dynamic-update-slice_fusion.4
  24.5 0.7 constant_dynamic-update-slice_fusion.3
  25.2 0.7 constant_dynamic-update-slice_fusion.2
  25.8 0.7 constant_dynamic-update-slice_fusion.1
  26.6 0.9 constant_dynamic-update-slice_fusion
  27.5 2.1 %dynamic-slice_reduce_fusion = bf16[99328]{0:T(1024)(128)(2,1)S(1)} fusion(bf16[1,198656]{1,0:T(2,128)(2,1)} %constant_dynamic-update-slice_fusion, s32[]{:T(128)S(6)} %select_n.135), kind=kLoop, calls=%fused_computation.53 | loop fusion | bytes 397316 | tf_op jit(solution)/shard_map/jit(_roll_dynamic)/dynamic_slice | solution.py:18
  29.6 1.0 reshape.439
  30.6 24.5 %scatter_custom_fusion = bf16[512,16]{1,0:T(8,128)(2,1)S(1)} fusion(s32[6208]{0:T(1024)S(1)} %fusion.97, bf16[6208,16]{1,0:T(8,128)(2,1)S(1)} %reshape.439, bf16[]{:T(256)} %constant.87.clone.1), kind=kCustom, calls=%fused_computation.197 | custom fusion | bytes 16386 | tf_op jit(solution)/shard_map/scatter | solution.py:120
  55.2 2.3 %collective-permute-start.3 = (bf16[3,1,32,16]{3,2,1,0:T(8,128)(2,1)S(1)}, bf16[3,1,32,16]{3,2,1,0:T(8,128)(2,1)S(1)}, u32[]{:S(2)}, u32[]{:S(2)}) collective-permute-start(bf16[3,1,32,16]{3,2,1,0:T(8,128)(2,1)S(1)} %get-tuple-element.84), channel_id=1, source_target_pairs={{0,4},{1,5},{2,6},{3,7},{8,12},{9,13},{10,14},{11,15},{16,20},{17,... | collective-permute-start | bytes 9224 | tf_op jit(solution)/shard_map/ppermute | solution.py:28
  57.5 1.3 collective-permute-start.4
  58.8 1.4 fusion.72
  60.3 1.8 %collective-permute-done.4 = bf16[3,1,32,16]{3,2,1,0:T(8,128)(2,1)S(1)} collective-permute-done((bf16[3,1,32,16]{3,2,1,0:T(8,128)(2,1)S(1)}, bf16[3,1,32,16]{3,2,1,0:T(8,128)(2,1)S(1)}, u32[]{:S(2)}, u32[]{:S(2)}) %collective-permute-start.4) | collective-permute-done | bytes 3104 | tf_op jit(solution)/shard_map/ppermute | solution.py:29
  62.3 6.5 %collective-permute-start.6 = (bf16[3,18,1,16]{3,2,1,0:T(2,128)(2,1)S(1)}, bf16[3,18,1,16]{3,2,1,0:T(2,128)(2,1)S(1)}, u32[]{:S(2)}, u32[]{:S(2)}) collective-permute-start(bf16[3,18,1,16]{3,2,1,0:T(2,128)(2,1)S(1)} %get-tuple-element.68), channel_id=1, source_target_pairs={{1,0},{2,1},{3,2},{5,4},{6,5},{7,6},{9,8},{10,9},{11,10},{13,12},{... | collective-permute-start | bytes 5192 | tf_op jit(solution)/shard_map/ppermute | solution.py:29
  69.2 4.6 %collective-permute-start.5 = (bf16[3,18,1,16]{3,2,1,0:T(2,128)(2,1)S(1)}, bf16[3,18,1,16]{3,2,1,0:T(2,128)(2,1)S(1)}, u32[]{:S(2)}, u32[]{:S(2)}) collective-permute-start(bf16[3,18,1,16]{3,2,1,0:T(2,128)(2,1)S(1)} %get-tuple-element.69), channel_id=1, source_target_pairs={{0,1},{1,2},{2,3},{4,5},{5,6},{6,7},{8,9},{9,10},{10,11},{12,13},{... | collective-permute-start | bytes 5192 | tf_op jit(solution)/shard_map/ppermute | solution.py:28
  76.3 0.6 constant_dynamic-update-slice_fusion.34
  79.5 0.6 multiply_reduce_fusion
  80.6 1.5 collective-permute-start.7
  82.1 1.3 collective-permute-start.8
  83.4 1.4 fusion.38
  84.8 2.4 %collective-permute-done.8 = bf16[3,1,32,384]{3,2,1,0:T(8,128)(2,1)S(1)} collective-permute-done((bf16[3,1,32,384]{3,2,1,0:T(8,128)(2,1)S(1)}, bf16[3,1,32,384]{3,2,1,0:T(8,128)(2,1)S(1)}, u32[]{:S(2)}, u32[]{:S(2)}) %collective-permute-start.8) | collective-permute-done | bytes 73760 | tf_op jit(solution)/shard_map/ppermute | solution.py:29
  87.6 1.4 fusion.78
  89.1 1.9 %collective-permute-start.10 = (bf16[3,18,1,384]{3,2,1,0:T(2,128)(2,1)S(1)}, bf16[3,18,1,384]{3,2,1,0:T(2,128)(2,1)S(1)}, u32[]{:S(2)}, u32[]{:S(2)}) collective-permute-start(bf16[3,18,1,384]{3,2,1,0:T(2,128)(2,1)S(1)} %get-tuple-element.35), channel_id=1, source_target_pairs={{1,0},{2,1},{3,2},{5,4},{6,5},{7,6},{9,8},{10,9},{11,10},{13,12},{... | collective-permute-start | bytes 124424 | tf_op jit(solution)/shard_map/ppermute | solution.py:29
  91.0 4.8 %collective-permute-start.9 = (bf16[3,18,1,384]{3,2,1,0:T(2,128)(2,1)S(1)}, bf16[3,18,1,384]{3,2,1,0:T(2,128)(2,1)S(1)}, u32[]{:S(2)}, u32[]{:S(2)}) collective-permute-start(bf16[3,18,1,384]{3,2,1,0:T(2,128)(2,1)S(1)} %get-tuple-element.34), channel_id=1, source_target_pairs={{0,1},{1,2},{2,3},{4,5},{5,6},{6,7},{8,9},{9,10},{10,11},{12,13},{... | collective-permute-start | bytes 124424 | tf_op jit(solution)/shard_map/ppermute | solution.py:28
  95.8 1.4 fusion.55
  97.2 1.4 fusion.61
  100.1 1.9 %maximum_maximum_fusion = (bf16[3,18,33,384]{3,2,1,0:T(8,128)(2,1)S(1)}, bf16[3,18,33,384]{3,2,1,0:T(8,128)(2,1)S(1)}) fusion(bf16[3,1,32,384]{3,2,1,0:T(8,128)(2,1)S(1)} %collective-permute-done.8, bf16[1,16,32,384]{3,2,1,0:T(8,128)(2,1)S(1)} %bitcast.186, bf16[2,16,32,384]{3,2,1,0:T(8,128)(2,1)S(1)} %copy-done.3, ...), kind=kLoop, calls=%fused_computation.13 | loop fusion | flops 13685760 | bytes 4147200 | tf_op jit(solution)/shard_map/concatenate | solution.py:30
  102.1 2.2 %fusion.101 = (bf16[1,16,32,384]{3,2,1,0:T(8,128)(2,1)}, bf16[1,16,32,384]{3,2,1,0:T(8,128)(2,1)}, bf16[1,16,32,384]{3,2,1,0:T(8,128)(2,1)S(1)}, bf16[1,16,32,38...) fusion(bf16[3,18,33,384]{3,2,1,0:T(8,128)(2,1)S(1)} %get-tuple-, ...), kind=kLoop, calls=%fused_computation.229 | loop fusion | bytes 14155776 | tf_op jit(solution)/shard_map/slice | solution.py:41
  111.3 0.8 fusion.13
  112.3 0.7 fusion.21
  113.3 0.6 fusion.28
  113.9 1.4 collective-permute-start.11
  115.4 1.3 collective-permute-start.12
  116.7 3.3 %collective-permute-done.12 = bf16[1,32,384]{2,1,0:T(8,128)(2,1)S(1)} collective-permute-done((bf16[1,32,384]{2,1,0:T(8,128)(2,1)S(1)}, bf16[1,32,384]{2,1,0:T(8,128)(2,1)S(1)}, u32[]{:S(2)}, u32[]{:S(2)}) %collective-permute-start.12) | collective-permute-done | bytes 24608 | tf_op jit(solution)/shard_map/ppermute | solution.py:29
  120.0 3.8 %collective-permute-start.13 = (bf16[18,1,384]{2,1,0:T(2,128)(2,1)S(1)}, bf16[18,1,384]{2,1,0:T(2,128)(2,1)S(1)}, u32[]{:S(2)}, u32[]{:S(2)}) collective-permute-start(bf16[18,1,384]{2,1,0:T(2,128)(2,1)S(1)} %get-tuple-element.48), channel_id=1, source_target_pairs={{0,1},{1,2},{2,3},{4,5},{5,6},{6,7},{8,9},{9,10},{10,11},{12,13},{... | collective-permute-start | bytes 41480 | tf_op jit(solution)/shard_map/ppermute | solution.py:28
  123.8 2.1 %collective-permute-start.14 = (bf16[18,1,384]{2,1,0:T(2,128)(2,1)S(1)}, bf16[18,1,384]{2,1,0:T(2,128)(2,1)S(1)}, u32[]{:S(2)}, u32[]{:S(2)}) collective-permute-start(bf16[18,1,384]{2,1,0:T(2,128)(2,1)S(1)} %get-tuple-element.49), channel_id=1, source_target_pairs={{1,0},{2,1},{3,2},{5,4},{6,5},{7,6},{9,8},{10,9},{11,10},{13,12},{... | collective-permute-start | bytes 41480 | tf_op jit(solution)/shard_map/ppermute | solution.py:29
  126.5 2.5 %collective-permute-done.14 = bf16[18,1,384]{2,1,0:T(2,128)(2,1)S(1)} collective-permute-done((bf16[18,1,384]{2,1,0:T(2,128)(2,1)S(1)}, bf16[18,1,384]{2,1,0:T(2,128)(2,1)S(1)}, u32[]{:S(2)}, u32[]{:S(2)}) %collective-permute-start.14) | collective-permute-done | bytes 13856 | tf_op jit(solution)/shard_map/ppermute | solution.py:29
  129.4 2.3 %broadcast_in_dim.42 = bf16[36,34,2,384]{3,2,1,0:T(2,128)(2,1)} broadcast(bf16[36,34,384]{2,1,0:T(8,128)(2,1)S(1)} %bitcast.198), dimensions={0,1,3} | broadcast | bytes 2820096 | tf_op jit(solution)/shard_map/broadcast_in_dim | solution.py:161
  131.6 4.2 %reshape.431 = bf16[36,68,384]{2,1,0:T(8,128)(2,1)S(1)} reshape(bf16[36,34,2,384]{3,2,1,0:T(2,128)(2,1)} %broadcast_in_dim.42) | data formatting | bytes 3760128 | tf_op jit(solution)/shard_map/reshape | solution.py:161
  135.8 0.9 slice_bitcast_fusion
  136.7 3.6 %fusion.100 = (bf16[1,32,64,384]{3,2,1,0:T(8,128)(2,1)S(1)}, bf16[1,32,64,384]{3,2,1,0:T(8,128)(2,1)S(1)}, bf16[1,32,64,384]{3,2,1,0:T(8,128)(2,1)S(1)}, bf16[1,...) fusion(bf16[1,34,66,384]{3,2,1,0:T(8,128)(2,1)S(1)} %slice_bitc, ...), kind=kLoop, calls=%fused_computation.228 | loop fusion | bytes 28311552 | tf_op jit(solution)/shard_map/slice | solution.py:41
  140.3 0.7 fusion.89
  141.0 0.7 convolution_add_fusion.7
  141.8 0.7 convolution_add_fusion.6
  142.5 0.7 convolution_add_fusion.5
  143.2 0.7 convolution_add_fusion.4
  143.9 0.7 convolution_add_fusion.3
  144.7 0.7 convolution_add_fusion.2
  145.4 0.7 convolution_add_fusion.1
  146.2 0.7 fusion.2
  147.4 2.0 %reshape.433 = bf16[1,32,12288]{2,1,0:T(8,128)(2,1)} reshape(bf16[2048,192]{1,0:T(8,128)(2,1)S(1)} %copy.50) | data formatting | bytes 1572864 | tf_op jit(solution)/shard_map/reshape | solution.py:167
  (183 shorter events, 19.2 us)
Async XLA Ops:
  0.0 79.5 %copy-start = (bf16[432,384]{1,0:T(8,128)(2,1)S(1)}, bf16[432,384]{1,0:T(8,128)(2,1)}, u32[]{:S(2)}) copy-start(bf16[432,384]{1,0:T(8,128)(2,1)} %param.17) | copy-start | bytes 995332
  0.0 12.9 %collective-permute-start = (bf16[1,12416]{1,0:T(2,128)(2,1)}, bf16[1,12416]{1,0:T(2,128)(2,1)S(1)}, u32[]{:S(2)}, u32[]{:S(2)}) collective-permute-start(bf16[1,12416]{1,0:T(2,128)(2,1)} %param.12), channel_id=1, source_target_pairs={{0,7},{1,0},{2,1},{3,2},{4,3},{5,4},{6,5},{7,6},{8,15},{9,8},{10,9... | collective-permute-start | bytes 74504 | tf_op jit(solution)/shard_map/ppermute | solution.py:14
  9.8 2.8 %copy-start.14 = (bf16[1,2,16,512]{3,2,1,0:T(8,128)(2,1)S(1)}, bf16[1,2,16,512]{3,2,1,0:T(8,128)(2,1)}, u32[]{:S(2)}) copy-start(bf16[1,2,16,512]{3,2,1,0:T(8,128)(2,1)} %param.15) | copy-start | bytes 98308
  11.1 1.8 %copy-start.13 = (bf16[1,12416]{1,0:T(2,128)(2,1)S(1)}, bf16[1,12416]{1,0:T(2,128)(2,1)}, u32[]{:S(2)}) copy-start(bf16[1,12416]{1,0:T(2,128)(2,1)} %param.12) | copy-start | bytes 74500
  12.0 15.4 %copy-start.2 = (bf16[2,16,32,384]{3,2,1,0:T(8,128)(2,1)}, bf16[2,16,32,384]{3,2,1,0:T(8,128)(2,1)S(1)}, u32[]{:S(2)}) copy-start(bf16[2,16,32,384]{3,2,1,0:T(8,128)(2,1)S(1)} %bitcast_multiply_fusion) | copy-start | bytes 2359300
  13.0 5.8 %collective-permute-start.1 = (bf16[1,24832]{1,0:T(2,128)(2,1)S(1)}, bf16[1,24832]{1,0:T(2,128)(2,1)S(1)}, u32[]{:S(2)}, u32[]{:S(2)}) collective-permute-start(bf16[1,24832]{1,0:T(2,128)(2,1)S(1)} %pad_maximum_fusion.18), channel_id=1, source_target_pairs={{0,6},{1,7},{2,0},{3,1},{4,2},{5,3},{6,4},{7,5},{8,14},{9,15},{10,... | collective-permute-start | bytes 149000 | tf_op jit(solution)/shard_map/ppermute | solution.py:14
  19.0 4.6 %collective-permute-start.2 = (bf16[1,49664]{1,0:T(2,128)(2,1)S(1)}, bf16[1,49664]{1,0:T(2,128)(2,1)S(1)}, u32[]{:S(2)}, u32[]{:S(2)}) collective-permute-start(bf16[1,49664]{1,0:T(2,128)(2,1)S(1)} %pad_maximum_fusion.11), channel_id=1, source_target_pairs={{0,4},{1,5},{2,6},{3,7},{4,0},{5,1},{6,2},{7,3},{8,12},{9,13},{10,... | collective-permute-start | bytes 297992 | tf_op jit(solution)/shard_map/ppermute | solution.py:14
  29.6 29.2 %slice-start = ((bf16[2,16,32,384]{3,2,1,0:T(8,128)(2,1)}), bf16[1,16,32,384]{3,2,1,0:T(8,128)(2,1)S(1)}, s32[]{:S(2)}) async-start(bf16[2,16,32,384]{3,2,1,0:T(8,128)(2,1)} %copy-done.2), calls=%async_computation | async-start | bytes 786432 | tf_op jit(solution)/shard_map/slice | solution.py:41
  55.2 5.1 %collective-permute-start.3 = (bf16[3,1,32,16]{3,2,1,0:T(8,128)(2,1)S(1)}, bf16[3,1,32,16]{3,2,1,0:T(8,128)(2,1)S(1)}, u32[]{:S(2)}, u32[]{:S(2)}) collective-permute-start(bf16[3,1,32,16]{3,2,1,0:T(8,128)(2,1)S(1)} %get-tuple-element.84), channel_id=1, source_target_pairs={{0,4},{1,5},{2,6},{3,7},{8,12},{9,13},{10,14},{11,15},{16,20},{17,... | collective-permute-start | bytes 9224 | tf_op jit(solution)/shard_map/ppermute | solution.py:28
  57.5 4.6 %collective-permute-start.4 = (bf16[3,1,32,16]{3,2,1,0:T(8,128)(2,1)S(1)}, bf16[3,1,32,16]{3,2,1,0:T(8,128)(2,1)S(1)}, u32[]{:S(2)}, u32[]{:S(2)}) collective-permute-start(bf16[3,1,32,16]{3,2,1,0:T(8,128)(2,1)S(1)} %get-tuple-element.85), channel_id=1, source_target_pairs={{4,0},{5,1},{6,2},{7,3},{12,8},{13,9},{14,10},{15,11},{20,16},{21,... | collective-permute-start | bytes 9224 | tf_op jit(solution)/shard_map/ppermute | solution.py:29
  62.3 12.3 %collective-permute-start.6 = (bf16[3,18,1,16]{3,2,1,0:T(2,128)(2,1)S(1)}, bf16[3,18,1,16]{3,2,1,0:T(2,128)(2,1)S(1)}, u32[]{:S(2)}, u32[]{:S(2)}) collective-permute-start(bf16[3,18,1,16]{3,2,1,0:T(2,128)(2,1)S(1)} %get-tuple-element.68), channel_id=1, source_target_pairs={{1,0},{2,1},{3,2},{5,4},{6,5},{7,6},{9,8},{10,9},{11,10},{13,12},{... | collective-permute-start | bytes 5192 | tf_op jit(solution)/shard_map/ppermute | solution.py:29
  69.2 6.3 %collective-permute-start.5 = (bf16[3,18,1,16]{3,2,1,0:T(2,128)(2,1)S(1)}, bf16[3,18,1,16]{3,2,1,0:T(2,128)(2,1)S(1)}, u32[]{:S(2)}, u32[]{:S(2)}) collective-permute-start(bf16[3,18,1,16]{3,2,1,0:T(2,128)(2,1)S(1)} %get-tuple-element.69), channel_id=1, source_target_pairs={{0,1},{1,2},{2,3},{4,5},{5,6},{6,7},{8,9},{9,10},{10,11},{12,13},{... | collective-permute-start | bytes 5192 | tf_op jit(solution)/shard_map/ppermute | solution.py:28
  77.2 2.0 %copy-start.18 = (bf16[512,432]{0,1:T(8,128)(2,1)S(1)}, bf16[512,432]{0,1:T(8,128)(2,1)}, u32[]{:S(2)}) copy-start(bf16[512,432]{0,1:T(8,128)(2,1)} %constant_dynamic-update-slice_fusion.34) | copy-start | bytes 1327108
  77.6 1.9 %copy-start.19 = (f32[384]{0:T(512)S(1)}, f32[384]{0:T(512)}, u32[]{:S(2)}) copy-start(f32[384]{0:T(512)} %param.18) | copy-start | bytes 4612
  78.9 1.2 copy-start.15
  79.5 1.1 copy-start.3
  80.1 18.4 %slice-start.1 = ((s8[7962624]{0:T(1024)(128)(4,1)}), s8[4194304]{0:T(1024)(128)(4,1)S(1)}, s32[]{:S(2)}) async-start(s8[7962624]{0:T(1024)(128)(4,1)} %bitcast.187), calls=%async_computation.1 | async-start | bytes 8388608
  80.6 4.2 %collective-permute-start.7 = (bf16[3,1,32,384]{3,2,1,0:T(8,128)(2,1)S(1)}, bf16[3,1,32,384]{3,2,1,0:T(8,128)(2,1)S(1)}, u32[]{:S(2)}, u32[]{:S(2)}) collective-permute-start(bf16[3,1,32,384]{3,2,1,0:T(8,128)(2,1)S(1)} %get-tuple-element.45), channel_id=1, source_target_pairs={{0,4},{1,5},{2,6},{3,7},{8,12},{9,13},{10,14},{11,15},{16,20},{17,... | collective-permute-start | bytes 221192 | tf_op jit(solution)/shard_map/ppermute | solution.py:28
  82.1 5.1 %collective-permute-start.8 = (bf16[3,1,32,384]{3,2,1,0:T(8,128)(2,1)S(1)}, bf16[3,1,32,384]{3,2,1,0:T(8,128)(2,1)S(1)}, u32[]{:S(2)}, u32[]{:S(2)}) collective-permute-start(bf16[3,1,32,384]{3,2,1,0:T(8,128)(2,1)S(1)} %get-tuple-element.46), channel_id=1, source_target_pairs={{4,0},{5,1},{6,2},{7,3},{12,8},{13,9},{14,10},{15,11},{20,16},{21,... | collective-permute-start | bytes 221192 | tf_op jit(solution)/shard_map/ppermute | solution.py:29
  84.8 13.8 %slice-start.2 = ((s8[7962624]{0:T(1024)(128)(4,1)}), s8[3768320]{0:T(1024)(128)(4,1)S(1)}, s32[]{:S(2)}) async-start(s8[7962624]{0:T(1024)(128)(4,1)} %bitcast.187), calls=%async_computation.2 | async-start | bytes 7536640
  89.1 11.0 %collective-permute-start.10 = (bf16[3,18,1,384]{3,2,1,0:T(2,128)(2,1)S(1)}, bf16[3,18,1,384]{3,2,1,0:T(2,128)(2,1)S(1)}, u32[]{:S(2)}, u32[]{:S(2)}) collective-permute-start(bf16[3,18,1,384]{3,2,1,0:T(2,128)(2,1)S(1)} %get-tuple-element.35), channel_id=1, source_target_pairs={{1,0},{2,1},{3,2},{5,4},{6,5},{7,6},{9,8},{10,9},{11,10},{13,12},{... | collective-permute-start | bytes 124424 | tf_op jit(solution)/shard_map/ppermute | solution.py:29
  91.0 9.1 %collective-permute-start.9 = (bf16[3,18,1,384]{3,2,1,0:T(2,128)(2,1)S(1)}, bf16[3,18,1,384]{3,2,1,0:T(2,128)(2,1)S(1)}, u32[]{:S(2)}, u32[]{:S(2)}) collective-permute-start(bf16[3,18,1,384]{3,2,1,0:T(2,128)(2,1)S(1)} %get-tuple-element.34), channel_id=1, source_target_pairs={{0,1},{1,2},{2,3},{4,5},{5,6},{6,7},{8,9},{9,10},{10,11},{12,13},{... | collective-permute-start | bytes 124424 | tf_op jit(solution)/shard_map/ppermute | solution.py:28
  107.4 1.0 copy-start.11
  107.8 1.0 copy-start.10
  108.2 1.1 copy-start.9
  108.8 1.0 copy-start.8
  109.3 1.0 copy-start.7
  110.3 1.0 copy-start.5
  111.3 1.0 copy-start.4
  112.3 1.0 copy-start.6
  112.3 1.0 copy-start.16
  113.9 2.7 %collective-permute-start.11 = (bf16[1,32,384]{2,1,0:T(8,128)(2,1)S(1)}, bf16[1,32,384]{2,1,0:T(8,128)(2,1)S(1)}, u32[]{:S(2)}, u32[]{:S(2)}) collective-permute-start(bf16[1,32,384]{2,1,0:T(8,128)(2,1)S(1)} %get-tuple-element.76), channel_id=1, source_target_pairs={{0,4},{1,5},{2,6},{3,7},{8,12},{9,13},{10,14},{11,15},{16,20},{17,... | collective-permute-start | bytes 73736 | tf_op jit(solution)/shard_map/ppermute | solution.py:28
  115.4 4.6 %collective-permute-start.12 = (bf16[1,32,384]{2,1,0:T(8,128)(2,1)S(1)}, bf16[1,32,384]{2,1,0:T(8,128)(2,1)S(1)}, u32[]{:S(2)}, u32[]{:S(2)}) collective-permute-start(bf16[1,32,384]{2,1,0:T(8,128)(2,1)S(1)} %get-tuple-element.77), channel_id=1, source_target_pairs={{4,0},{5,1},{6,2},{7,3},{12,8},{13,9},{14,10},{15,11},{20,16},{21,... | collective-permute-start | bytes 73736 | tf_op jit(solution)/shard_map/ppermute | solution.py:29
  120.0 6.5 %collective-permute-start.13 = (bf16[18,1,384]{2,1,0:T(2,128)(2,1)S(1)}, bf16[18,1,384]{2,1,0:T(2,128)(2,1)S(1)}, u32[]{:S(2)}, u32[]{:S(2)}) collective-permute-start(bf16[18,1,384]{2,1,0:T(2,128)(2,1)S(1)} %get-tuple-element.48), channel_id=1, source_target_pairs={{0,1},{1,2},{2,3},{4,5},{5,6},{6,7},{8,9},{9,10},{10,11},{12,13},{... | collective-permute-start | bytes 41480 | tf_op jit(solution)/shard_map/ppermute | solution.py:28
  123.8 5.2 %collective-permute-start.14 = (bf16[18,1,384]{2,1,0:T(2,128)(2,1)S(1)}, bf16[18,1,384]{2,1,0:T(2,128)(2,1)S(1)}, u32[]{:S(2)}, u32[]{:S(2)}) collective-permute-start(bf16[18,1,384]{2,1,0:T(2,128)(2,1)S(1)} %get-tuple-element.49), channel_id=1, source_target_pairs={{1,0},{2,1},{3,2},{5,4},{6,5},{7,6},{9,8},{10,9},{11,10},{13,12},{... | collective-permute-start | bytes 41480 | tf_op jit(solution)/shard_map/ppermute | solution.py:29
  136.7 3.6 %copy-start.12 = (bf16[3456,192]{0,1:T(8,128)(2,1)S(1)}, bf16[3456,192]{0,1:T(8,128)(2,1)}, u32[]{:S(2)}) copy-start(bf16[3456,192]{0,1:T(8,128)(2,1)} %param.22) | copy-start | bytes 3981316
  145.4 0.7 copy-start.17
  146.2 3.3 %copy-start.1 = (bf16[432,384]{1,0:T(8,128)(2,1)S(1)}, bf16[432,384]{1,0:T(8,128)(2,1)}, u32[]{:S(2)}) copy-start(bf16[432,384]{1,0:T(8,128)(2,1)} %param.17) | copy-start | bytes 995332
